TPU v7x, 512 devices: a whole 4x4x16 slice. The times are simulated.
512 devices in a mesh: row: 16 (over z), col: 32 (over y, x, core).
Axes of the slice: x: 4, y: 4, z: 16, core: 2. Of those that a mesh axis runs over, the one named last changes fastest.
Arguments:
- left_rows: float32 [2, 2048, 65536], P(None, 'row', 'col'), may hold values from -0.0234375 to 0.0234375
- prior_solution: float32 [65536, 128], P('col'), may hold values from -6 to 6
- diag_rhs: float32 [2, 2048, 128], P(None, 'row'), may hold values from -6 to 6
- inverse_blocks: float32 [2, 2048, 2048], P(None, 'col', 'row'), may hold values from -0.125 to 0.125
- sub_block_t: float32 [2048, 2048], P('col', 'row'), may hold values from -0.125 to 0.125
- trail_panel_t: float32 [2, 2048, 16384], P(None, 'col', 'row'), may hold values from -0.09375 to 0.09375
- trail_rhs: float32 [16384, 128], P(('row', 'col')), may hold values from -6 to 6
Outputs:
- solved: float32 [2, 2048, 128], P(None, 'col')
- trail_out: float32 [16384, 128], P(('row', 'col'))
All inputs are finite; a program needn't handle non-finite values.
Results may differ from a plain program's by a relative error of at most 0.000082.
Values sent between devices are 32-bit elements; how exact they have to be, the bound alone decides.
A program may use at most 64 MiB of HBM per device.

v0:
```python
import jax
import jax.numpy as jnp
from jax import lax
from jax.sharding import PartitionSpec as P


def solve_block(residue, inverse_piece, block_index):
    precise = lax.Precision.HIGHEST
    height = inverse_piece.shape[1]
    narrow = inverse_piece.shape[2]
    row_start = lax.axis_index("col") * height
    row_ids = row_start + lax.broadcasted_iota(jnp.int32, (height, 1), 0)
    col_start = lax.axis_index("row") * narrow
    col_ids = col_start + lax.broadcasted_iota(jnp.int32, (1, narrow), 1)
    masked = jnp.where(row_ids >= col_ids, inverse_piece[block_index], 0.0)
    partial_solve = jnp.dot(masked, residue, precision=precise)
    return lax.psum(partial_solve, "row")


def on_device(
    left_rows, prior_solution, diag_rhs, inverse_blocks, sub_block_t, trail_panel_t, trail_rhs
):
    precise = lax.Precision.HIGHEST
    partial_left = jnp.einsum("knj,jr->knr", left_rows, prior_solution, precision=precise)
    summed = lax.psum(partial_left, "col")
    residue_first = diag_rhs[0] - summed[0]
    residue_pending = diag_rhs[1] - summed[1]
    first = solve_block(residue_first, inverse_blocks, 0)
    sub_partial = lax.dot_general(sub_block_t, first, (((0,), (0,)), ((), ())), precision=precise)
    update = lax.psum(sub_partial, "col")
    residue_second = residue_pending - update
    second = solve_block(residue_second, inverse_blocks, 1)
    solved = jnp.stack([first, second])
    trail_partial = jnp.einsum("knt,knr->tr", trail_panel_t, solved, precision=precise)
    share = lax.psum_scatter(trail_partial, "col", scatter_dimension=0, tiled=True)
    return (solved, trail_rhs - share)


def solution(mesh):
    in_specs = (
        P(None, "row", "col"),
        P("col", None),
        P(None, "row", None),
        P(None, "col", "row"),
        P("col", "row"),
        P(None, "col", "row"),
        P(("row", "col"), None),
    )
    out_specs = (P(None, "col", None), P(("row", "col"), None))
    return jax.shard_map(
        on_device, mesh=mesh, in_specs=in_specs, out_specs=out_specs, check_vma=False
    )
```

profile of v0, /device:TPU:1, one launch (start us, length us, event | category | flops | bytes accessed | tf_op | source)
XLA Modules:
  0.0 491.2 jit_solution(12153111198170251669)
XLA Ops:
  7.2 0.0 copy-start
  7.2 0.0 all-reduce.3.cloned.1.call-start
  7.3 1.5 copy-done
  8.8 3.7 fusion
  12.4 0.0 all-reduce.3.cloned.1.call-update
  12.5 0.0 all-reduce.5.cloned.1.call-start
  12.5 135.8 %all-reduce.3.cloned.1.call-done = f32[2,128,128]{2,1,0:T(8,128)} async-done(((f32[2,128,128]{2,1,0:T(8,128)}), f32[2,128,128]{2,1,0:T(8,128)}) %all-reduce.3.cloned.1.call-update) | async-done | bytes 131088 | tf_op jit(solution)/shard_map/psum | solution.py:25
  148.4 0.0 copy-done.3
  148.4 1.1 fusion.6
  149.5 43.0 %psum.29 = f32[64,128]{1,0:T(8,128)S(1)} all-reduce(f32[64,128]{1,0:T(8,128)S(1)} %fusion.6), channel_id=1, replica_groups=mesh['row'=16,'col'=32] {'row'}, use_global_device_ids=true, to_apply=%region_1.2 | all-reduce | flops 8192 | bytes 65536 | tf_op jit(solution)/shard_map/psum | solution.py:17
  192.5 0.9 convolution_bitcast_fusion.1
  193.4 0.0 all-reduce.5.cloned.1.call-update
  193.5 0.0 reduce-scatter.4.cloned.1.call-start
  193.5 136.4 %all-reduce.5.cloned.1.call-done = f32[128,128]{1,0:T(8,128)} async-done(((f32[128,128]{1,0:T(8,128)}), f32[128,128]{1,0:T(8,128)}) %all-reduce.5.cloned.1.call-update) | async-done | bytes 65552 | tf_op jit(solution)/shard_map/psum | solution.py:30
  329.9 1.1 convolution_bitcast_fusion.2
  331.0 43.7 %psum.31 = f32[1,64,128]{2,1,0:T(8,128)S(1)} all-reduce(f32[1,64,128]{2,1,0:T(8,128)S(1)} %convolution_bitcast_fusion.2), channel_id=1, replica_groups=mesh['row'=16,'col'=32] {'row'}, use_global_device_ids=true, to_apply=%region_3.4 | all-reduce | flops 8192 | bytes 65536 | tf_op jit(solution)/shard_map/psum | solution.py:17
  374.7 0.0 copy-start.2
  374.7 0.6 convolution_bitcast_fusion
  375.3 1.0 copy.13
  376.3 0.0 reduce-scatter.4.cloned.1.call-update
  376.3 0.1 copy.11
  376.4 106.8 %reduce-scatter.4.cloned.1.call-done = f32[32,128]{1,0:T(8,128)} async-done(((f32[1024,128]{1,0:T(8,128)}), f32[32,128]{1,0:T(8,128)}) %reduce-scatter.4.cloned.1.call-update) | async-done | bytes 16400
  483.2 0.8 copy.14
  484.0 0.7 copy.12
  (14 shorter events, 0.0 us)
Async XLA Ops:
  7.2 1.6 copy-start
  7.2 141.2 %copy-start.4 = (f32[2,64,128]{2,1,0:T(8,128)S(1)}, f32[2,64,128]{2,1,0:T(8,128)}, u32[]{:S(2)}) copy-start(f32[2,64,128]{2,1,0:T(8,128)} %param.10) | copy-start | bytes 196612
  7.2 141.2 %copy-start.3 = (f32[2,128,128]{2,1,0:T(8,128)S(1)}, f32[2,128,128]{2,1,0:T(8,128)}, u32[]{:S(2)}) copy-start(f32[2,128,128]{2,1,0:T(8,128)} %param.9) | copy-start | bytes 393220
  7.2 185.3 %copy-start.5 = (f32[64,128]{1,0:T(8,128)S(1)}, f32[64,128]{1,0:T(8,128)}, u32[]{:S(2)}) copy-start(f32[64,128]{1,0:T(8,128)} %param.11) | copy-start | bytes 98308
  7.2 367.4 %copy-start.1 = (f32[2,64,1024]{2,1,0:T(8,128)S(1)}, f32[2,64,1024]{2,1,0:T(8,128)}, u32[]{:S(2)}) copy-start(f32[2,64,1024]{2,1,0:T(8,128)} %param.12) | copy-start | bytes 1572868
  7.2 141.2 %all-reduce.3.cloned.1.call-start = ((), (), s32[]{:S(2)}) async-start(), calls=%async_computation.1 | async-start | bytes 262144 | tf_op jit(solution)/shard_map/psum | solution.py:25
  12.4 363.9 %copy-start.6 = (f32[32,128]{1,0:T(8,128)S(1)}, f32[32,128]{1,0:T(8,128)}, u32[]{:S(2)}) copy-start(f32[32,128]{1,0:T(8,128)} %param.13) | copy-start | bytes 49156
  12.5 317.4 %all-reduce.5.cloned.1.call-start = ((), (), s32[]{:S(2)}) async-start(), calls=%async_computation.2 | async-start | bytes 131072 | tf_op jit(solution)/shard_map/psum | solution.py:30
  193.5 289.7 %reduce-scatter.4.cloned.1.call-start = ((), (), s32[]{:S(2)}) async-start(), calls=%async_computation.3 | async-start | bytes 540672
  374.7 110.1 %copy-start.2 = (f32[2,64,128]{2,1,0:T(8,128)}, f32[2,64,128]{2,1,0:T(8,128)S(1)}, u32[]{:S(2)}) copy-start(f32[2,64,128]{2,1,0:T(8,128)S(1)} %pad_maximum_fusion) | copy-start | bytes 196612
Sparse Core Ops, SparseCore 0:
  12.6 135.7 all-reduce.2
  193.6 136.2 all-reduce.4
  376.4 106.7 reduce-scatter.3
where the time goes:
time: 492 us; the launch traced here: 491 us
  waiting for transfers between devices  379 us (77%)
  blocking collectives  86.7 us (18%)
  between operations  13.9 us (3%)
  matrix products  7.41 us (2%)
    psum x1, waiting for transfers between devices, on_device(): update = lax.psum(sub_partial, 'col')  136 us
    psum x1, waiting for transfers between devices, on_device(): summed = lax.psum(partial_left, 'col')  136 us
    unnamed x4, waiting for transfers between devices  107 us
    psum x2, blocking collectives, solve_block(): return lax.psum(partial_solve, 'row')  86.7 us
  transfers between devices with their start and end apart: 3, of which 3 were waited for; matrix products, arithmetic and copies ran while one was open for 0% of the time, Pallas kernels for 0%

commit v1 on v0

v1 whole, which is shorter than its diff:
```python
import jax
import jax.numpy as jnp
from jax import lax
from jax.experimental import pallas as pl
from jax.experimental.pallas import tpu as pltpu
from jax.sharding import PartitionSpec as P


F32 = jnp.float32
BF16 = jnp.bfloat16
MESH = pl.DeviceIdType.MESH
NZ = 16
CHUNKS = 4
WINDOW = 8


def ring4(d):
    return min(d, 4 - d)


CHIPS = sorted(((dy, dx) for dy in range(4) for dx in range(4)), key=lambda o: (-(ring4(o[0]) + ring4(o[1])), o))
FAR_Z = sorted(range(1, NZ), key=lambda d: -min(d, NZ - d))


def split(x):
    high = x.astype(BF16)
    return high, (x - high.astype(F32)).astype(BF16)


def dot(a, b):
    return jnp.dot(a, b, preferred_element_type=F32)


def tree_sum(terms):
    terms = list(terms)
    while len(terms) > 1:
        paired = [terms[i] + terms[i + 1] for i in range(0, len(terms) - 1, 2)]
        if len(terms) % 2:
            paired.append(terms[-1])
        terms = paired
    return terms[0]


def kernel(
    left, prior, diag, inverse, sub, panel, rhs, solved_ref, out_ref,
    left_v, prior_v, diag_v, inverse_v, sub_g, low_g, panel_v, rhs_v,
    prior_w, diag_t, part0, part1, red0, red1, res0, res1, res1_in, low0_h, low0_l,
    first_s, first_z, first_g, sub_h, sub_l, upd_s, upd_r, x_t, low1_w, second_z,
    panel_w, sib_s, sib_r, trail_s, trail_r,
    load_sem, chunk_sem, send_sem, recv_sem, sib_sem,
):
    r = lax.axis_index("row")
    c = lax.axis_index("col")
    y, x, k = c // 8, (c // 2) % 4, c % 2
    q = c // 2
    ys = [(y + d) % 4 for d in range(4)]
    xs = [(x + d) % 4 for d in range(4)]
    zs = [(r + d) % NZ for d in range(NZ)]

    def chip(o):
        return ys[o[0]] * 4 + xs[o[1]]

    src_row = (r + NZ - 4 + q // 2) % NZ
    src_chip = 2 * (r % 8) + q % 2
    ahead = (r - q // 2 + 4 + NZ) % NZ
    dst_row = q // 2 + 8 * (ahead // 8)
    dst_chip = 2 * (ahead % 8) + q % 2
    away = jnp.logical_or(dst_row != r, dst_chip != q)

    step = prior.shape[0] // CHUNKS
    for i in range(CHUNKS):
        rows = pl.ds(i * step, step)
        pltpu.make_async_copy(prior.at[rows, :], prior_v.at[rows, :], chunk_sem.at[0, i]).start()
        pltpu.make_async_copy(left.at[0, :, rows], left_v.at[0, :, rows], chunk_sem.at[1, i]).start()
    loads = [
        pltpu.make_async_copy(left.at[1], left_v.at[1], load_sem.at[0]),
        pltpu.make_async_copy(diag.at[k], diag_v, load_sem.at[1]),
        pltpu.make_async_copy(inverse, inverse_v, load_sem.at[2]),
        pltpu.make_async_copy(sub, sub_g.at[4], load_sem.at[3]),
        pltpu.make_async_copy(panel, panel_v, load_sem.at[4]),
        pltpu.make_async_copy(rhs, rhs_v, load_sem.at[5]),
    ]
    for copy in loads:
        copy.start()

    barrier = pltpu.get_barrier_semaphore()

    def greet(row, col):
        pl.semaphore_signal(barrier, inc=1, device_id=(row, col), device_id_type=MESH)

    for d in FAR_Z:
        greet(zs[d], c)
    for o in CHIPS:
        greet(r, 2 * chip(o) + (1 - k))
        if o != (0, 0):
            greet(r, 2 * chip(o) + k)

    @pl.when(jnp.logical_and(k == 1, away))
    def _():
        greet(src_row, 2 * src_chip + 1)

    def remote(src, dst, number, row, col):
        pltpu.make_async_remote_copy(
            src_ref=src, dst_ref=dst, send_sem=send_sem.at[number], recv_sem=recv_sem.at[number],
            device_id=(row, col), device_id_type=MESH,
        ).start()

    def received(ref, number):
        pltpu.make_async_copy(ref, ref, recv_sem.at[number]).wait()

    def sent(ref, number):
        pltpu.make_async_copy(ref, ref, send_sem.at[number]).wait()

    def to_reducers(src, dst, core, number):
        for o in CHIPS[:-1]:
            remote(src.at[chip(o)], dst.at[2 * (4 * o[0] + o[1]) + k], number, r, 2 * chip(o) + core)

        @pl.when(k != core)
        def _():
            remote(src.at[q], dst.at[k], number, r, 2 * q + core)

        @pl.when(k == core)
        def _():
            dst[core] = src[q]

    def to_reducers_sent(ref, core, number):
        @pl.when(k == core)
        def _():
            sent(ref.at[pl.ds(0, 15)], number)

        @pl.when(k != core)
        def _():
            sent(ref, number)

    def from_reducer(ref, core, number):
        for o in CHIPS:
            remote(ref.at[q], ref.at[q], number, r, 2 * chip(o) + (1 - core))
            if o != (0, 0):
                remote(ref.at[q], ref.at[q], number, r, 2 * chip(o) + core)

    def from_reducers_received(ref, core, number):
        @pl.when(k == core)
        def _():
            received(ref.at[pl.ds(0, 15)], number)

        @pl.when(k != core)
        def _():
            received(ref, number)

    def window(ref, slot, number):
        for w in (0, 1, 7, 2, 6, 3, 5):
            to = slot(w)
            remote(ref.at[slot(4)], ref.at[to], number, zs[(4 - w) % NZ], c)

    def left_product(b, parts):
        total = None
        for i in parts:
            rows = pl.ds(i * step, step)
            if b == 0:
                pltpu.make_async_copy(prior.at[rows, :], prior_v.at[rows, :], chunk_sem.at[0, i]).wait()
                prior_w[rows, :] = jnp.concatenate(split(prior_v[rows, :]), axis=1)
                pltpu.make_async_copy(left.at[0, :, rows], left_v.at[0, :, rows], chunk_sem.at[1, i]).wait()
            high, low = split(left_v[b, :, rows])
            wide = dot(high, prior_w[rows, :])
            term = wide[:, :128] + wide[:, 128:] + dot(low, prior_w[rows, :128])
            total = term if total is None else total + term
        return total.T.reshape(16, 8, 128)

    part0[...] = left_product(0, range(CHUNKS))

    pl.semaphore_wait(barrier, 46 + jnp.where(jnp.logical_and(k == 1, away), 1, 0))

    to_reducers(part0, red0, 0, 0)

    loads[3].wait()
    window(sub_g, lambda w: w, 4)

    loads[0].wait()
    part1[...] = left_product(1, range(CHUNKS))
    to_reducers(part1, red1, 1, 1)

    loads[1].wait()
    diag_t[...] = diag_v[...].T.reshape(16, 8, 128)
    loads[2].wait()
    row_ids = c * 64 + lax.broadcasted_iota(jnp.int32, (64, 128), 0)
    col_ids = r * 128 + lax.broadcasted_iota(jnp.int32, (64, 128), 1)
    keep = row_ids >= col_ids
    low0 = jnp.where(keep, inverse_v[0], 0.0)
    nothing = jnp.zeros((64, 128), F32)
    high, low = split(
        jnp.concatenate(
            [jnp.concatenate([low0, nothing], axis=1), jnp.concatenate([nothing, low0], axis=1)], axis=0
        ).T
    )
    low0_h[...] = high
    low0_l[...] = low
    low_g[4] = jnp.where(keep, inverse_v[1], 0.0)

    @pl.when(k == 0)
    def _():
        received(red0.at[pl.ds(0, 31)], 0)
        res0[q] = diag_t[q] - tree_sum(red0[i] for i in range(32))
        from_reducer(res0, 0, 2)

    @pl.when(k == 1)
    def _():
        received(red1.at[pl.ds(0, 31)], 1)
        mine = diag_t[q] - tree_sum(red1[i] for i in range(32))

        @pl.when(away)
        def _():
            res1[...] = mine
            remote(res1, res1_in, 3, dst_row, 2 * dst_chip + 1)

        @pl.when(jnp.logical_not(away))
        def _():
            res1_in[...] = mine

    to_reducers_sent(part0, 0, 0)
    to_reducers_sent(part1, 1, 1)
    from_reducers_received(res0, 0, 2)

    even = jnp.concatenate([res0[2 * i] for i in range(8)], axis=0)
    odd = jnp.concatenate([res0[2 * i + 1] for i in range(8)], axis=0)
    high, low = split(jnp.concatenate([even, odd], axis=1))
    both = dot(jnp.concatenate([high, low], axis=0), low0_h[...])
    first_s[...] = (both[:64] + both[64:] + dot(high, low0_l[...])).reshape(8, 8, 128)
    for d in FAR_Z:
        remote(first_s.at[zs[d] % 8], first_z.at[d], 5, zs[d], c)
    window(low_g, lambda w: w, 6)
    group = r % 8

    loads[4].wait()
    for i in range(8):
        block = panel_v[:, :, 128 * i:128 * (i + 1)].reshape(128, 128).T
        panel_w[4 * i:4 * (i + 1)] = jnp.concatenate(split(block), axis=1).reshape(4, 32, 256)
    received(sub_g.at[pl.ds(0, 7)], 4)
    for w in range(WINDOW):
        high, low = split(sub_g[w])
        sub_h[:, 128 * w:128 * (w + 1)] = high
        sub_l[:, 128 * w:128 * (w + 1)] = low

    @pl.when(k == 0)
    def _():
        sent(red0.at[pl.ds(0, 31)], 2)

    @pl.when(jnp.logical_and(k == 1, away))
    def _():
        sent(res1, 3)
        received(res1_in, 3)

    received(first_z.at[pl.ds(0, 15)], 5)
    first = first_s[group] + tree_sum(first_z[d] for d in range(1, NZ))
    first_g[group] = first

    high, low = split(jnp.concatenate([first[:, :64], first[:, 64:]], axis=0))
    both = dot(jnp.concatenate([high, low], axis=0), sub_h[...])
    update = both[:16] + both[16:] + dot(high, sub_l[...])
    for w in range(WINDOW):
        for h in range(2):
            upd_s[2 * w + h] = update[8 * h:8 * (h + 1), 128 * w:128 * (w + 1)]
    to_reducers(upd_s, upd_r, 1, 7)

    for w in (0, 1, 7, 2, 6, 3, 5):
        remote(first_g.at[group], first_g.at[group], 8, zs[(4 - w) % NZ], c)
    sent(first_z.at[pl.ds(0, 15)], 5)
    sent(sub_g.at[pl.ds(0, 7)], 4)

    @pl.when(k == 1)
    def _():
        received(upd_r.at[pl.ds(0, 31)], 7)
        x_t[q] = res1_in[...] - tree_sum(upd_r[i] for i in range(32))
        from_reducer(x_t, 1, 9)

    received(low_g.at[pl.ds(0, 7)], 6)
    for w in range(WINDOW):
        high, low = split(low_g[w])
        stacked = jnp.concatenate([high.astype(F32), low.astype(F32)], axis=0).T
        low1_w[128 * w:128 * (w + 1), :] = stacked.astype(BF16)
    to_reducers_sent(upd_s, 1, 7)
    sent(low_g.at[pl.ds(0, 7)], 6)
    received(first_g.at[pl.ds(0, 7)], 8)
    sent(first_g.at[pl.ds(0, 7)], 8)
    from_reducers_received(x_t, 1, 9)

    upper = jnp.concatenate([x_t[2 * w] for w in range(WINDOW)], axis=1)
    under = jnp.concatenate([x_t[2 * w + 1] for w in range(WINDOW)], axis=1)
    high, low = split(jnp.concatenate([upper, under], axis=0))
    both = dot(jnp.concatenate([high, low], axis=0), low1_w[...])
    both = both[:16] + both[16:]
    both = both + pltpu.roll(both, 64, 1)
    left_half = lax.broadcasted_iota(jnp.int32, (8, 128), 1) < 64
    second_z[r] = jnp.where(left_half, both[:8], both[8:])
    for d in FAR_Z:
        remote(second_z.at[r], second_z.at[r], 10, zs[d], c)

    @pl.when(k == 1)
    def _():
        sent(upd_r.at[pl.ds(0, 31)], 9)

    received(second_z.at[pl.ds(0, 15)], 10)
    rows = []
    for g in range(8):
        a = first_g[g]
        b = second_z[g] + second_z[g + 8]
        rows.append(jnp.where(left_half, a, pltpu.roll(b, 64, 1)))
        rows.append(jnp.where(left_half, pltpu.roll(a, 64, 1), b))
    solved = jnp.concatenate(rows, axis=0).T
    solved_ref[...] = solved.reshape(2, 64, 128)

    high, low = split(solved)
    weights = jnp.concatenate(
        [jnp.concatenate([high, low], axis=1), jnp.concatenate([high, jnp.zeros((128, 128), BF16)], axis=1)], axis=0
    )

    def trail(group, core):
        lines = jnp.concatenate([panel_w[2 * chip(o) + core] for o in group], axis=0)
        wide = dot(lines, weights)
        return wide[:, :128] + wide[:, 128:]

    groups = [CHIPS[4 * i:4 * (i + 1)] for i in range(4)]
    for i, group in enumerate(groups):
        sib_s[i] = trail(group, 1 - k)
        pltpu.make_async_remote_copy(
            src_ref=sib_s.at[i], dst_ref=sib_r.at[i], send_sem=send_sem.at[11], recv_sem=sib_sem.at[i],
            device_id=(r, 2 * q + (1 - k)), device_id_type=MESH,
        ).start()
    for i, group in enumerate(groups):
        mine = trail(group, k)
        pltpu.make_async_copy(sib_r.at[i], sib_r.at[i], sib_sem.at[i]).wait()
        mine = mine + sib_r[i]
        for j, o in enumerate(group):
            slot = 4 * o[0] + o[1]
            if slot:
                trail_s[slot] = mine[32 * j:32 * (j + 1)]
                remote(trail_s.at[slot], trail_r.at[slot], 12, r, 2 * chip(o) + k)
            else:
                trail_r[0] = mine[32 * j:32 * (j + 1)]
    sent(second_z.at[pl.ds(0, 15)], 10)
    sent(sib_s, 11)
    loads[5].wait()
    received(trail_r.at[pl.ds(0, 15)], 12)
    out_ref[...] = rhs_v[...] - tree_sum(trail_r[i] for i in range(16))
    sent(trail_s.at[pl.ds(0, 15)], 12)


def on_device(*args):
    left, prior, diag, inverse, sub, panel, rhs = args
    tiles = lambda n: pltpu.VMEM((n, 8, 128), F32)
    return pl.pallas_call(
        kernel,
        out_shape=(
            jax.ShapeDtypeStruct((2, 64, 128), F32),
            jax.ShapeDtypeStruct((32, 128), F32),
        ),
        in_specs=[pl.BlockSpec(memory_space=pl.ANY)] * 7,
        out_specs=(pl.BlockSpec(memory_space=pltpu.VMEM), pl.BlockSpec(memory_space=pltpu.VMEM)),
        scratch_shapes=[
            pltpu.VMEM((2, 128, 2048), F32),
            pltpu.VMEM((2048, 128), F32),
            pltpu.VMEM((128, 128), F32),
            pltpu.VMEM((2, 64, 128), F32),
            pltpu.VMEM((WINDOW, 64, 128), F32),
            pltpu.VMEM((WINDOW, 64, 128), F32),
            pltpu.VMEM((2, 64, 1024), F32),
            pltpu.VMEM((32, 128), F32),
            pltpu.VMEM((2048, 256), BF16),
            tiles(16),
            tiles(16),
            tiles(16),
            tiles(32),
            tiles(32),
            tiles(16),
            pltpu.VMEM((8, 128), F32),
            pltpu.VMEM((8, 128), F32),
            pltpu.VMEM((256, 128), BF16),
            pltpu.VMEM((256, 128), BF16),
            tiles(8),
            tiles(16),
            tiles(8),
            pltpu.VMEM((64, 1024), BF16),
            pltpu.VMEM((64, 1024), BF16),
            tiles(16),
            tiles(32),
            tiles(16),
            pltpu.VMEM((1024, 128), BF16),
            tiles(16),
            pltpu.VMEM((32, 32, 256), BF16),
            pltpu.VMEM((4, 128, 128), F32),
            pltpu.VMEM((4, 128, 128), F32),
            pltpu.VMEM((16, 32, 128), F32),
            pltpu.VMEM((16, 32, 128), F32),
            pltpu.SemaphoreType.DMA((6,)),
            pltpu.SemaphoreType.DMA((2, CHUNKS)),
            pltpu.SemaphoreType.DMA((13,)),
            pltpu.SemaphoreType.DMA((13,)),
            pltpu.SemaphoreType.DMA((4,)),
        ],
        compiler_params=pltpu.CompilerParams(
            collective_id=0, has_side_effects=True, vmem_limit_bytes=48 * 1024 * 1024
        ),
    )(left, prior, diag, inverse, sub, panel, rhs)


def solution(mesh):
    in_specs = (
        P(None, "row", "col"),
        P("col", None),
        P(None, "row", None),
        P(None, "col", "row"),
        P("col", "row"),
        P(None, "col", "row"),
        P(("row", "col"), None),
    )
    out_specs = (P(None, "col", None), P(("row", "col"), None))
    return jax.shard_map(
        on_device, mesh=mesh, in_specs=in_specs, out_specs=out_specs, check_vma=False
    )
```

time: 492 us -> 69.2 us (0.14)
  waiting for transfers between devices: 379 us -> 0 us
  blocking collectives: 86.7 us -> 0 us
  Pallas kernels: 0 us -> 59.8 us
  between operations: 13.9 us -> 0.66 us
  matrix products: 7.41 us -> 0 us
    psum x2 -> x0, waiting for transfers between devices: 272 us -> none  [the longest x1 136 us: on_device(): update = lax.psum(sub_partial, 'col')]
    unnamed x4 -> x0, waiting for transfers between devices: 107 us -> none
    psum x2 -> x0, blocking collectives: 86.7 us -> none  [solve_block(): return lax.psum(partial_solve, 'row')]
    pallas_call x0 -> x1, Pallas kernels: none -> 59.8 us  [on_device(): pl.pallas_call(kernel, out_shape=(jax.ShapeDtypeStruct((2, 64, 128), F32)...]
    dot_general x5 -> x0, matrix products: 7.41 us -> none  [the longest x1 3.68 us: on_device(): jnp.einsum('knj,jr->knr', left_rows, prior_solution, precision=precise)]
  transfers between devices with their start and end apart: 3 -> 0, of which waited for: 3 -> 0; matrix products, arithmetic and copies ran while one was open for 0% -> 0% of each run, Pallas kernels for 0% -> 0%
where the time goes in v1:
time: 69.2 us; the launch traced here: 68.7 us
  Pallas kernels  59.8 us (86%)
  local copies, waits for them, and re-layouts  8.3 us (12%)
    pallas_call x1, Pallas kernels, on_device(): pl.pallas_call(kernel, out_shape=(jax.ShapeDtypeStruct((2, 64, 128), F32)...  59.8 us
    unnamed x16, local copies, waits for them, and re-layouts  8.3 us

profile of v1, /device:TPU:1, one launch (start us, length us, event | category | flops | bytes accessed | tf_op | source)
XLA Modules:
  0.0 68.7 jit_solution(75002082309708396)
XLA Ops:
  0.6 0.0 copy-start
  0.6 1.6 %copy-done = f32[2,128,2048]{2,1,0:T(8,128)S(1)} copy-done((f32[2,128,2048]{2,1,0:T(8,128)S(1)}, f32[2,128,2048]{2,1,0:T(8,128)}, u32[]{:S(2)}) %copy-start) | copy-done | bytes 2097176
  2.2 0.0 copy-start.1
  2.2 1.2 %copy-done.1 = f32[2048,128]{1,0:T(8,128)S(1)} copy-done((f32[2048,128]{1,0:T(8,128)S(1)}, f32[2048,128]{1,0:T(8,128)}, u32[]{:S(2)}) %copy-start.1) | copy-done | bytes 1048600
  3.4 0.0 copy-start.2
  3.5 1.0 %copy-done.2 = f32[2,64,1024]{2,1,0:T(8,128)S(1)} copy-done((f32[2,64,1024]{2,1,0:T(8,128)S(1)}, f32[2,64,1024]{2,1,0:T(8,128)}, u32[]{:S(2)}) %copy-start.2) | copy-done | bytes 524312
  4.5 0.0 copy-start.3
  4.5 0.9 %copy-done.3 = f32[2,128,128]{2,1,0:T(8,128)S(1)} copy-done((f32[2,128,128]{2,1,0:T(8,128)S(1)}, f32[2,128,128]{2,1,0:T(8,128)}, u32[]{:S(2)}) %copy-start.3) | copy-done | bytes 131096
  5.4 0.0 copy-start.4
  5.4 0.8 %copy-done.4 = f32[2,64,128]{2,1,0:T(8,128)S(1)} copy-done((f32[2,64,128]{2,1,0:T(8,128)S(1)}, f32[2,64,128]{2,1,0:T(8,128)}, u32[]{:S(2)}) %copy-start.4) | copy-done | bytes 65560
  6.2 0.0 copy-start.5
  6.2 0.8 %copy-done.5 = f32[64,128]{1,0:T(8,128)S(1)} copy-done((f32[64,128]{1,0:T(8,128)S(1)}, f32[64,128]{1,0:T(8,128)}, u32[]{:S(2)}) %copy-start.5) | copy-done | bytes 32792
  7.0 0.0 copy-start.6
  7.0 0.7 %copy-done.6 = f32[32,128]{1,0:T(8,128)S(1)} copy-done((f32[32,128]{1,0:T(8,128)S(1)}, f32[32,128]{1,0:T(8,128)}, u32[]{:S(2)}) %copy-start.6) | copy-done | bytes 16408
  7.7 59.8 %shard_map.86 = (f32[2,64,128]{2,1,0:T(8,128)S(1)}, f32[32,128]{1,0:T(8,128)S(1)}) custom-call(f32[2,128,2048]{2,1,0:T(8,128)S(1)} %copy-done, f32[2048,128]{1,0:T(8,128)S(1)} %copy-done.1, f32[2,128,128]{2,1,0:T(8,128)S(1)} %copy-done.3, f32[2,64,128]{2,1,0:T(8,128)S(1)} %copy-done.4, f32[64,128]{1,0:T(8,128)S(1)} %copy-done.5, ...), custom_call_target="tpu_custom_call" | custom-call | tf_op jit(solution)/shard_map/pallas_call | solution.py:350
  67.5 0.6 copy.11
  68.1 0.6 copy.12
Async XLA Ops:
  0.6 1.6 %copy-start = (f32[2,128,2048]{2,1,0:T(8,128)S(1)}, f32[2,128,2048]{2,1,0:T(8,128)}, u32[]{:S(2)}) copy-start(f32[2,128,2048]{2,1,0:T(8,128)} %left.1) | copy-start | bytes 6291460
  2.2 1.2 %copy-start.1 = (f32[2048,128]{1,0:T(8,128)S(1)}, f32[2048,128]{1,0:T(8,128)}, u32[]{:S(2)}) copy-start(f32[2048,128]{1,0:T(8,128)} %prior.1) | copy-start | bytes 3145732
  3.4 1.0 %copy-start.2 = (f32[2,64,1024]{2,1,0:T(8,128)S(1)}, f32[2,64,1024]{2,1,0:T(8,128)}, u32[]{:S(2)}) copy-start(f32[2,64,1024]{2,1,0:T(8,128)} %panel.1) | copy-start | bytes 1572868
  4.5 0.9 %copy-start.3 = (f32[2,128,128]{2,1,0:T(8,128)S(1)}, f32[2,128,128]{2,1,0:T(8,128)}, u32[]{:S(2)}) copy-start(f32[2,128,128]{2,1,0:T(8,128)} %diag.1) | copy-start | bytes 393220
  5.4 0.8 %copy-start.4 = (f32[2,64,128]{2,1,0:T(8,128)S(1)}, f32[2,64,128]{2,1,0:T(8,128)}, u32[]{:S(2)}) copy-start(f32[2,64,128]{2,1,0:T(8,128)} %inverse.1) | copy-start | bytes 196612
  6.2 0.8 %copy-start.5 = (f32[64,128]{1,0:T(8,128)S(1)}, f32[64,128]{1,0:T(8,128)}, u32[]{:S(2)}) copy-start(f32[64,128]{1,0:T(8,128)} %sub.1) | copy-start | bytes 98308
  7.0 0.7 %copy-start.6 = (f32[32,128]{1,0:T(8,128)S(1)}, f32[32,128]{1,0:T(8,128)}, u32[]{:S(2)}) copy-start(f32[32,128]{1,0:T(8,128)} %rhs.1) | copy-start | bytes 49156

commit v2 on v1

--- a/solution.py
+++ b/solution.py
@@ -19,6 +19,7 @@
 
 
 CHIPS = sorted(((dy, dx) for dy in range(4) for dx in range(4)), key=lambda o: (-(ring4(o[0]) + ring4(o[1])), o))
+NEAR_Z = (4, 12, 3, 13, 2, 14, 1, 15)
 FAR_Z = sorted(range(1, NZ), key=lambda d: -min(d, NZ - d))
 
 
@@ -47,7 +48,7 @@
     prior_w, diag_t, part0, part1, red0, red1, res0, res1, res1_in, low0_h, low0_l,
     first_s, first_z, first_g, sub_h, sub_l, upd_s, upd_r, x_t, low1_w, second_z,
     panel_w, sib_s, sib_r, trail_s, trail_r,
-    load_sem, chunk_sem, send_sem, recv_sem, sib_sem,
+    load_sem, chunk_sem, send_sem, recv_sem, sib_sem, passed_sem,
 ):
     r = lax.axis_index("row")
     c = lax.axis_index("col")
@@ -60,8 +61,6 @@
     def chip(o):
         return ys[o[0]] * 4 + xs[o[1]]
 
-    src_row = (r + NZ - 4 + q // 2) % NZ
-    src_chip = 2 * (r % 8) + q % 2
     ahead = (r - q // 2 + 4 + NZ) % NZ
     dst_row = q // 2 + 8 * (ahead // 8)
     dst_chip = 2 * (ahead % 8) + q % 2
@@ -80,24 +79,23 @@
         pltpu.make_async_copy(panel, panel_v, load_sem.at[4]),
         pltpu.make_async_copy(rhs, rhs_v, load_sem.at[5]),
     ]
-    for copy in loads:
-        copy.start()
 
     barrier = pltpu.get_barrier_semaphore()
 
     def greet(row, col):
         pl.semaphore_signal(barrier, inc=1, device_id=(row, col), device_id_type=MESH)
 
-    for d in FAR_Z:
+    for o in CHIPS[:5]:
+        greet(r, 2 * chip(o) + (1 - k))
+        greet(r, 2 * chip(o) + k)
+    for d in NEAR_Z:
         greet(zs[d], c)
-    for o in CHIPS:
+    for o in CHIPS[5:]:
         greet(r, 2 * chip(o) + (1 - k))
         if o != (0, 0):
             greet(r, 2 * chip(o) + k)
-
-    @pl.when(jnp.logical_and(k == 1, away))
-    def _():
-        greet(src_row, 2 * src_chip + 1)
+    for copy in loads:
+        copy.start()
 
     def remote(src, dst, number, row, col):
         pltpu.make_async_remote_copy(
@@ -168,16 +166,14 @@
 
     part0[...] = left_product(0, range(CHUNKS))
 
-    pl.semaphore_wait(barrier, 46 + jnp.where(jnp.logical_and(k == 1, away), 1, 0))
+    pl.semaphore_wait(barrier, 39)
 
     to_reducers(part0, red0, 0, 0)
+    for d in NEAR_Z:
+        pl.semaphore_signal(passed_sem, inc=1, device_id=(zs[d], c), device_id_type=MESH)
 
     loads[3].wait()
     window(sub_g, lambda w: w, 4)
-
-    loads[0].wait()
-    part1[...] = left_product(1, range(CHUNKS))
-    to_reducers(part1, red1, 1, 1)
 
     loads[1].wait()
     diag_t[...] = diag_v[...].T.reshape(16, 8, 128)
@@ -202,22 +198,10 @@
         res0[q] = diag_t[q] - tree_sum(red0[i] for i in range(32))
         from_reducer(res0, 0, 2)
 
-    @pl.when(k == 1)
-    def _():
-        received(red1.at[pl.ds(0, 31)], 1)
-        mine = diag_t[q] - tree_sum(red1[i] for i in range(32))
-
-        @pl.when(away)
-        def _():
-            res1[...] = mine
-            remote(res1, res1_in, 3, dst_row, 2 * dst_chip + 1)
-
-        @pl.when(jnp.logical_not(away))
-        def _():
-            res1_in[...] = mine
-
+    loads[0].wait()
+    part1[...] = left_product(1, range(CHUNKS))
+    to_reducers(part1, red1, 1, 1)
     to_reducers_sent(part0, 0, 0)
-    to_reducers_sent(part1, 1, 1)
     from_reducers_received(res0, 0, 2)
 
     even = jnp.concatenate([res0[2 * i] for i in range(8)], axis=0)
@@ -225,11 +209,27 @@
     high, low = split(jnp.concatenate([even, odd], axis=1))
     both = dot(jnp.concatenate([high, low], axis=0), low0_h[...])
     first_s[...] = (both[:64] + both[64:] + dot(high, low0_l[...])).reshape(8, 8, 128)
+    pl.semaphore_wait(passed_sem, 8)
     for d in FAR_Z:
         remote(first_s.at[zs[d] % 8], first_z.at[d], 5, zs[d], c)
     window(low_g, lambda w: w, 6)
     group = r % 8
 
+    @pl.when(k == 1)
+    def _():
+        received(red1.at[pl.ds(0, 31)], 1)
+        mine = diag_t[q] - tree_sum(red1[i] for i in range(32))
+
+        @pl.when(away)
+        def _():
+            res1[...] = mine
+            remote(res1, res1_in, 3, dst_row, 2 * dst_chip + 1)
+
+        @pl.when(jnp.logical_not(away))
+        def _():
+            res1_in[...] = mine
+
+    to_reducers_sent(part1, 1, 1)
     loads[4].wait()
     for i in range(8):
         block = panel_v[:, :, 128 * i:128 * (i + 1)].reshape(128, 128).T
@@ -395,9 +395,10 @@
             pltpu.SemaphoreType.DMA((13,)),
             pltpu.SemaphoreType.DMA((13,)),
             pltpu.SemaphoreType.DMA((4,)),
+            pltpu.SemaphoreType.REGULAR,
         ],
         compiler_params=pltpu.CompilerParams(
-            collective_id=0, has_side_effects=True, vmem_limit_bytes=48 * 1024 * 1024
+            collective_id=0, has_side_effects=True, vmem_limit_bytes=60 * 1024 * 1024
         ),
     )(left, prior, diag, inverse, sub, panel, rhs)
 

time: 69.2 us -> 66 us (0.954)
  local copies, waits for them, and re-layouts: 8.3 us -> 2.8 us
  Pallas kernels: 59.8 us -> 62.3 us
    unnamed x16 -> x2, local copies, waits for them, and re-layouts: 8.3 us -> 2.8 us
    pallas_call x1, Pallas kernels: 59.8 us -> 62.3 us  [on_device(): pl.pallas_call(kernel, out_shape=(jax.ShapeDtypeStruct((2, 64, 128), F32)...]
where the time goes in v2:
time: 66 us; the launch traced here: 65.7 us
  Pallas kernels  62.3 us (94%)
  local copies, waits for them, and re-layouts  2.8 us (4%)
    pallas_call x1, Pallas kernels, on_device(): pl.pallas_call(kernel, out_shape=(jax.ShapeDtypeStruct((2, 64, 128), F32)...  62.3 us
    unnamed x2, local copies, waits for them, and re-layouts  2.8 us

profile of v2, /device:TPU:1, one launch (start us, length us, event | category | flops | bytes accessed | tf_op | source)
XLA Modules:
  0.0 65.7 jit_solution(6267796598960826958)
XLA Ops:
  0.6 62.3 %shard_map.86 = (f32[2,64,128]{2,1,0:T(8,128)}, f32[32,128]{1,0:T(8,128)}) custom-call(f32[2,128,2048]{2,1,0:T(8,128)} %left.1, f32[2048,128]{1,0:T(8,128)} %prior.1, f32[2,128,128]{2,1,0:T(8,128)} %diag.1, f32[2,64,128]{2,1,0:T(8,128)} %inverse.1, f32[64,128]{1,0:T(8,128)} %sub.1, f32[2,64,1024]{2,1,0:T(8,128)} %panel.1, f32[32,128]{1,0:T(8,128)} %rhs.1), custom_call_target="tpu_custom_call" | custom-call | tf_op jit(solution)/shard_map/pallas_call | solution.py:350
  62.9 1.5 %copy.11 = f32[2,64,128]{2,1,0:T(8,128)} copy(f32[2,64,128]{2,1,0:T(8,128)} %get-tuple-element.4) | data formatting | bytes 131072
  64.4 1.3 %copy.12 = f32[32,128]{1,0:T(8,128)} copy(f32[32,128]{1,0:T(8,128)} %get-tuple-element.5) | data formatting | bytes 32768

commit v3 on v2

--- a/solution.py
+++ b/solution.py
@@ -12,6 +12,7 @@
 NZ = 16
 CHUNKS = 4
 WINDOW = 8
+SUB, LOW = 13, 15
 
 
 def ring4(d):
@@ -43,8 +44,8 @@
 
 
 def kernel(
-    left, prior, diag, inverse, sub, panel, rhs, solved_ref, out_ref,
-    left_v, prior_v, diag_v, inverse_v, sub_g, low_g, panel_v, rhs_v,
+    left, prior, diag, inverse, sub, panel, solved_ref, share_ref,
+    left_v, prior_v, diag_v, inverse_v, sub_g, low_g, panel_v,
     prior_w, diag_t, part0, part1, red0, red1, res0, res1, res1_in, low0_h, low0_l,
     first_s, first_z, first_g, sub_h, sub_l, upd_s, upd_r, x_t, low1_w, second_z,
     panel_w, sib_s, sib_r, trail_s, trail_r,
@@ -77,7 +78,6 @@
         pltpu.make_async_copy(inverse, inverse_v, load_sem.at[2]),
         pltpu.make_async_copy(sub, sub_g.at[4], load_sem.at[3]),
         pltpu.make_async_copy(panel, panel_v, load_sem.at[4]),
-        pltpu.make_async_copy(rhs, rhs_v, load_sem.at[5]),
     ]
 
     barrier = pltpu.get_barrier_semaphore()
@@ -145,10 +145,20 @@
         def _():
             received(ref, number)
 
-    def window(ref, slot, number):
-        for w in (0, 1, 7, 2, 6, 3, 5):
-            to = slot(w)
-            remote(ref.at[slot(4)], ref.at[to], number, zs[(4 - w) % NZ], c)
+    def window_start(ref, number):
+        for w in (2, 6, 3, 5):
+            remote(ref.at[4], ref.at[w], number, zs[(4 - w) % NZ], c)
+
+    def window_hand_on(ref, number):
+        received(ref.at[pl.ds(0, 4)], number)
+        remote(ref.at[2], ref.at[0], number + 1, zs[2], c)
+        remote(ref.at[2], ref.at[1], number + 1, zs[1], c)
+        remote(ref.at[6], ref.at[7], number + 1, zs[15], c)
+
+    def window_end(ref, number):
+        received(ref.at[pl.ds(0, 3)], number + 1)
+        sent(ref.at[pl.ds(0, 4)], number)
+        sent(ref.at[pl.ds(0, 3)], number + 1)
 
     def left_product(b, parts):
         total = None
@@ -173,14 +183,15 @@
         pl.semaphore_signal(passed_sem, inc=1, device_id=(zs[d], c), device_id_type=MESH)
 
     loads[3].wait()
-    window(sub_g, lambda w: w, 4)
-
-    loads[1].wait()
-    diag_t[...] = diag_v[...].T.reshape(16, 8, 128)
+    window_start(sub_g, SUB)
     loads[2].wait()
     row_ids = c * 64 + lax.broadcasted_iota(jnp.int32, (64, 128), 0)
     col_ids = r * 128 + lax.broadcasted_iota(jnp.int32, (64, 128), 1)
     keep = row_ids >= col_ids
+    low_g[4] = jnp.where(keep, inverse_v[1], 0.0)
+    window_start(low_g, LOW)
+    loads[1].wait()
+    diag_t[...] = diag_v[...].T.reshape(16, 8, 128)
     low0 = jnp.where(keep, inverse_v[0], 0.0)
     nothing = jnp.zeros((64, 128), F32)
     high, low = split(
@@ -190,7 +201,9 @@
     )
     low0_h[...] = high
     low0_l[...] = low
-    low_g[4] = jnp.where(keep, inverse_v[1], 0.0)
+
+    loads[0].wait()
+    part1[...] = left_product(1, range(CHUNKS))
 
     @pl.when(k == 0)
     def _():
@@ -198,9 +211,9 @@
         res0[q] = diag_t[q] - tree_sum(red0[i] for i in range(32))
         from_reducer(res0, 0, 2)
 
-    loads[0].wait()
-    part1[...] = left_product(1, range(CHUNKS))
     to_reducers(part1, red1, 1, 1)
+    window_hand_on(sub_g, SUB)
+    window_hand_on(low_g, LOW)
     to_reducers_sent(part0, 0, 0)
     from_reducers_received(res0, 0, 2)
 
@@ -212,7 +225,6 @@
     pl.semaphore_wait(passed_sem, 8)
     for d in FAR_Z:
         remote(first_s.at[zs[d] % 8], first_z.at[d], 5, zs[d], c)
-    window(low_g, lambda w: w, 6)
     group = r % 8
 
     @pl.when(k == 1)
@@ -234,20 +246,20 @@
     for i in range(8):
         block = panel_v[:, :, 128 * i:128 * (i + 1)].reshape(128, 128).T
         panel_w[4 * i:4 * (i + 1)] = jnp.concatenate(split(block), axis=1).reshape(4, 32, 256)
-    received(sub_g.at[pl.ds(0, 7)], 4)
+    window_end(sub_g, SUB)
     for w in range(WINDOW):
         high, low = split(sub_g[w])
         sub_h[:, 128 * w:128 * (w + 1)] = high
         sub_l[:, 128 * w:128 * (w + 1)] = low
+    window_end(low_g, LOW)
+    for w in range(WINDOW):
+        high, low = split(low_g[w])
+        stacked = jnp.concatenate([high.astype(F32), low.astype(F32)], axis=0).T
+        low1_w[128 * w:128 * (w + 1), :] = stacked.astype(BF16)
 
     @pl.when(k == 0)
     def _():
         sent(red0.at[pl.ds(0, 31)], 2)
-
-    @pl.when(jnp.logical_and(k == 1, away))
-    def _():
-        sent(res1, 3)
-        received(res1_in, 3)
 
     received(first_z.at[pl.ds(0, 15)], 5)
     first = first_s[group] + tree_sum(first_z[d] for d in range(1, NZ))
@@ -264,21 +276,19 @@
     for w in (0, 1, 7, 2, 6, 3, 5):
         remote(first_g.at[group], first_g.at[group], 8, zs[(4 - w) % NZ], c)
     sent(first_z.at[pl.ds(0, 15)], 5)
-    sent(sub_g.at[pl.ds(0, 7)], 4)
 
     @pl.when(k == 1)
     def _():
+        @pl.when(away)
+        def _():
+            sent(res1, 3)
+            received(res1_in, 3)
+
         received(upd_r.at[pl.ds(0, 31)], 7)
         x_t[q] = res1_in[...] - tree_sum(upd_r[i] for i in range(32))
         from_reducer(x_t, 1, 9)
 
-    received(low_g.at[pl.ds(0, 7)], 6)
-    for w in range(WINDOW):
-        high, low = split(low_g[w])
-        stacked = jnp.concatenate([high.astype(F32), low.astype(F32)], axis=0).T
-        low1_w[128 * w:128 * (w + 1), :] = stacked.astype(BF16)
     to_reducers_sent(upd_s, 1, 7)
-    sent(low_g.at[pl.ds(0, 7)], 6)
     received(first_g.at[pl.ds(0, 7)], 8)
     sent(first_g.at[pl.ds(0, 7)], 8)
     from_reducers_received(x_t, 1, 9)
@@ -338,22 +348,19 @@
                 trail_r[0] = mine[32 * j:32 * (j + 1)]
     sent(second_z.at[pl.ds(0, 15)], 10)
     sent(sib_s, 11)
-    loads[5].wait()
     received(trail_r.at[pl.ds(0, 15)], 12)
-    out_ref[...] = rhs_v[...] - tree_sum(trail_r[i] for i in range(16))
+    share_ref[...] = tree_sum(trail_r[i] for i in range(16))
     sent(trail_s.at[pl.ds(0, 15)], 12)
 
 
 def on_device(*args):
     left, prior, diag, inverse, sub, panel, rhs = args
     tiles = lambda n: pltpu.VMEM((n, 8, 128), F32)
-    return pl.pallas_call(
+    left, prior, diag, inverse, sub, panel = (pltpu.with_memory_space_constraint(a, pltpu.HBM) for a in (left, prior, diag, inverse, sub, panel))
+    solved, share = pl.pallas_call(
         kernel,
-        out_shape=(
-            jax.ShapeDtypeStruct((2, 64, 128), F32),
-            jax.ShapeDtypeStruct((32, 128), F32),
-        ),
-        in_specs=[pl.BlockSpec(memory_space=pl.ANY)] * 7,
+        out_shape=(jax.ShapeDtypeStruct((2, 64, 128), F32), jax.ShapeDtypeStruct((32, 128), F32)),
+        in_specs=[pl.BlockSpec(memory_space=pltpu.HBM)] * 6,
         out_specs=(pl.BlockSpec(memory_space=pltpu.VMEM), pl.BlockSpec(memory_space=pltpu.VMEM)),
         scratch_shapes=[
             pltpu.VMEM((2, 128, 2048), F32),
@@ -363,7 +370,6 @@
             pltpu.VMEM((WINDOW, 64, 128), F32),
             pltpu.VMEM((WINDOW, 64, 128), F32),
             pltpu.VMEM((2, 64, 1024), F32),
-            pltpu.VMEM((32, 128), F32),
             pltpu.VMEM((2048, 256), BF16),
             tiles(16),
             tiles(16),
@@ -390,17 +396,18 @@
             pltpu.VMEM((4, 128, 128), F32),
             pltpu.VMEM((16, 32, 128), F32),
             pltpu.VMEM((16, 32, 128), F32),
-            pltpu.SemaphoreType.DMA((6,)),
+            pltpu.SemaphoreType.DMA((5,)),
             pltpu.SemaphoreType.DMA((2, CHUNKS)),
-            pltpu.SemaphoreType.DMA((13,)),
-            pltpu.SemaphoreType.DMA((13,)),
+            pltpu.SemaphoreType.DMA((17,)),
+            pltpu.SemaphoreType.DMA((17,)),
             pltpu.SemaphoreType.DMA((4,)),
             pltpu.SemaphoreType.REGULAR,
         ],
         compiler_params=pltpu.CompilerParams(
-            collective_id=0, has_side_effects=True, vmem_limit_bytes=60 * 1024 * 1024
+            collective_id=0, has_side_effects=True, vmem_limit_bytes=32 * 1024 * 1024
         ),
-    )(left, prior, diag, inverse, sub, panel, rhs)
+    )(left, prior, diag, inverse, sub, panel)
+    return solved, rhs - share
 
 
 def solution(mesh):

time: 66 us -> 57.9 us (0.88)
  Pallas kernels: 62.3 us -> 55.8 us
  local copies, waits for them, and re-layouts: 2.8 us -> 0.63 us
    pallas_call x1, Pallas kernels: 62.3 us -> 55.8 us  [on_device(): pl.pallas_call(kernel, out_shape=(jax.ShapeDtypeStruct((2, 64, 128), F32)...]
    unnamed x2 -> x3, local copies, waits for them, and re-layouts: 2.8 us -> 0.63 us
where the time goes in v3:
time: 57.9 us; the launch traced here: 57.7 us
  Pallas kernels  55.8 us (96%)
  between operations  0.66 us (1%)
  local copies, waits for them, and re-layouts  0.63 us (1%)
  other arithmetic  0.61 us (1%)
    pallas_call x1, Pallas kernels, on_device(): pl.pallas_call(kernel, out_shape=(jax.ShapeDtypeStruct((2, 64, 128), F32)...  55.8 us

profile of v3, /device:TPU:1, one launch (start us, length us, event | category | flops | bytes accessed | tf_op | source)
XLA Modules:
  0.0 57.7 jit_solution(5766245355501622395)
XLA Ops:
  0.6 0.0 copy-start
  0.6 55.8 %shard_map.86 = (f32[2,64,128]{2,1,0:T(8,128)S(1)}, f32[32,128]{1,0:T(8,128)S(1)}) custom-call(f32[2,128,2048]{2,1,0:T(8,128)} %left.1, f32[2048,128]{1,0:T(8,128)} %prior.1, f32[2,128,128]{2,1,0:T(8,128)} %diag.1, f32[2,64,128]{2,1,0:T(8,128)} %inverse.1, f32[64,128]{1,0:T(8,128)} %sub.5, f32[2,64,1024]{2,1,0:T(8,128)} %panel.1), custom_call_target="tpu_custom_call" | custom-call | tf_op jit(solution)/shard_map/pallas_call | solution.py:360
  56.5 0.0 copy-done
  56.5 0.6 %sub.4 = f32[32,128]{1,0:T(8,128)} subtract(f32[32,128]{1,0:T(8,128)S(1)} %copy-done, f32[32,128]{1,0:T(8,128)S(1)} %get-tuple-element.5) | non-fusion elementwise | flops 4096 | bytes 49152 | tf_op jit(solution)/shard_map/sub | solution.py:410
  57.1 0.6 %copy.10 = f32[2,64,128]{2,1,0:T(8,128)} copy(f32[2,64,128]{2,1,0:T(8,128)S(1)} %get-tuple-element.8) | data formatting | bytes 131072
Async XLA Ops:
  0.6 55.8 %copy-start = (f32[32,128]{1,0:T(8,128)S(1)}, f32[32,128]{1,0:T(8,128)}, u32[]{:S(2)}) copy-start(f32[32,128]{1,0:T(8,128)} %param.13) | copy-start | bytes 49156

commit v4 on v0

v4 whole, which is shorter than its diff:
```python
import jax
import jax.numpy as jnp
from jax import lax
from jax.experimental import pallas as pl
from jax.experimental.pallas import tpu as pltpu
from jax.sharding import PartitionSpec as P


F32 = jnp.float32
BF16 = jnp.bfloat16
MESH = pl.DeviceIdType.MESH
NZ = 16
CHUNKS = 2
WINDOW = 8
RED0, RED1, RES0, RES1, FIRST, UPDATE, GROUP, SOLVE, SECOND, TRAIL, PANEL, LOW0, ROWS, SUB, LOW = *range(13), 13, 15


def ring4(d):
    return min(d, 4 - d)


CHIPS = sorted(((dy, dx) for dy in range(4) for dx in range(4)), key=lambda o: (-(ring4(o[0]) + ring4(o[1])), o))
NEAR_Z = (2, 14, 1, 15)
FAR_Z = sorted(range(1, NZ), key=lambda d: -min(d, NZ - d))


def split(x):
    high = x.astype(BF16)
    return high, (x - high.astype(F32)).astype(BF16)


def dot(a, b):
    return jnp.dot(a, b, preferred_element_type=F32)


def tree_sum(terms):
    terms = list(terms)
    while len(terms) > 1:
        paired = [terms[i] + terms[i + 1] for i in range(0, len(terms) - 1, 2)]
        if len(terms) % 2:
            paired.append(terms[-1])
        terms = paired
    return terms[0]


def kernel(
    left, prior, diag, inverse, sub, panel, solved_ref, share_ref,
    left_v, prior_v, diag_v, inverse_v, sub_g, low_g, low0_v, panel_v,
    prior_w, diag_t, part0, part1, red0, red1, res0, res1, res1_in,
    first_s, first_z, first_o, first_g, sub_h, sub_l, upd_s, upd_r, x_t, low1_w, second_s, second_z,
    panel_w, rows_s, rows_r, trail_s, trail_r,
    load_sem, chunk_sem, send_sem, recv_sem, passed_sem,
):
    r = lax.axis_index("row")
    c = lax.axis_index("col")
    y, x, k = c // 8, (c // 2) % 4, c % 2
    q = c // 2
    ys = [(y + d) % 4 for d in range(4)]
    xs = [(x + d) % 4 for d in range(4)]
    zs = [(r + d) % NZ for d in range(NZ)]
    group = r % 8
    half = group // 4
    mine = pl.ds(pl.multiple_of(64 * k, 64), 64)
    theirs = pl.ds(pl.multiple_of(64 * (1 - k), 64), 64)
    other = 2 * q + (1 - k)

    def chip(o):
        return ys[o[0]] * 4 + xs[o[1]]

    ahead = (r - q // 2 + 4 + NZ) % NZ
    dst_row = q // 2 + 8 * (ahead // 8)
    dst_chip = 2 * (ahead % 8) + q % 2
    away = jnp.logical_or(dst_row != r, dst_chip != q)

    step = prior.shape[0] // CHUNKS
    for i in range(CHUNKS):
        rows = pl.ds(i * step, step)
        pltpu.make_async_copy(prior.at[rows, :], prior_v.at[rows, :], chunk_sem.at[0, i]).start()
        pltpu.make_async_copy(left.at[0, :, rows], left_v.at[0, :, rows], chunk_sem.at[1, i]).start()
    loads = [
        pltpu.make_async_copy(left.at[1], left_v.at[1], load_sem.at[0]),
        pltpu.make_async_copy(diag, diag_v, load_sem.at[1]),
        pltpu.make_async_copy(inverse, inverse_v, load_sem.at[2]),
        pltpu.make_async_copy(sub, sub_g.at[4, mine], load_sem.at[3]),
        pltpu.make_async_copy(panel, panel_v.at[k], load_sem.at[4]),
    ]

    barrier = pltpu.get_barrier_semaphore()

    def greet(row, col):
        pl.semaphore_signal(barrier, inc=1, device_id=(row, col), device_id_type=MESH)

    @pl.when(k == 0)
    def _():
        for o in CHIPS:
            greet(r, 2 * chip(o) + 1)
            if o != (0, 0):
                greet(r, 2 * chip(o))
        for d in NEAR_Z:
            greet(zs[d], c)
            greet(zs[d], c + 1)

    @pl.when(k == 1)
    def _():
        greet(r, c - 1)

    for copy in loads:
        copy.start()

    def remote(src, dst, number, row, col):
        pltpu.make_async_remote_copy(
            src_ref=src, dst_ref=dst, send_sem=send_sem.at[number], recv_sem=recv_sem.at[number],
            device_id=(row, col), device_id_type=MESH,
        ).start()

    def received(tiles, number):
        size = prior_v.at[pl.ds(0, 8 * tiles)]
        pltpu.make_async_copy(size, size, recv_sem.at[number]).wait()

    def sent(tiles, number):
        size = prior_v.at[pl.ds(0, 8 * tiles)]
        pltpu.make_async_copy(size, size, send_sem.at[number]).wait()

    def to_reducers(src, dst, number, both):
        for o in CHIPS[:-1]:
            slot = 4 * o[0] + o[1]
            remote(src.at[chip(o)], dst.at[2 * slot + k if both else slot], number, r, 2 * chip(o))
        if both:

            @pl.when(k == 1)
            def _():
                remote(src.at[q], dst.at[1], number, r, 2 * q)

        @pl.when(k == 0)
        def _():
            dst[0] = src[q]

    def from_reducer(ref, number):
        for o in CHIPS[:-1]:
            remote(ref.at[q], ref.at[q], number, r, 2 * chip(o))

    def window_start(ref, number):
        for w in (2, 6, 3, 5):
            remote(ref.at[4, mine], ref.at[w, mine], number, zs[(4 - w) % NZ], 2 * q)

        @pl.when(k == 1)
        def _():
            remote(ref.at[4, mine], ref.at[4, mine], number, r, 2 * q)

    def window_hand_on(ref, number):
        received(72, number)
        remote(ref.at[2], ref.at[0], number + 1, zs[2], c)
        remote(ref.at[2], ref.at[1], number + 1, zs[1], c)
        remote(ref.at[6], ref.at[7], number + 1, zs[15], c)

    def left_product(b):
        total = None
        for i in range(CHUNKS):
            rows = pl.ds(i * step, step)
            if b == 0:
                pltpu.make_async_copy(prior.at[rows, :], prior_v.at[rows, :], chunk_sem.at[0, i]).wait()
                prior_w[rows, :] = jnp.concatenate(split(prior_v[rows, :]), axis=1)
                pltpu.make_async_copy(left.at[0, :, rows], left_v.at[0, :, rows], chunk_sem.at[1, i]).wait()
            wide = dot(jnp.concatenate(split(left_v[b, :, rows]), axis=0), prior_w[rows, :])
            total = wide if total is None else total + wide
        return chunks(total[:128, :128] + total[:128, 128:] + total[128:, :128])

    def chunks(product):
        return product.T.reshape(16, 8, 128)

    part0[...] = left_product(0)

    pl.semaphore_wait(barrier, 20)

    to_reducers(part0, red0, RED0, True)

    def pass_on(number, distance):
        for d in (distance, NZ - distance):
            pl.semaphore_signal(passed_sem.at[number], inc=1, device_id=(zs[d], c), device_id_type=MESH)

    @pl.when(k == 0)
    def _():
        pass_on(0, 2)

    loads[3].wait()
    window_start(sub_g, SUB)
    loads[2].wait()
    row_ids = c * 64 + lax.broadcasted_iota(jnp.int32, (64, 128), 0)
    col_ids = r * 128 + lax.broadcasted_iota(jnp.int32, (64, 128), 1)
    keep = row_ids >= col_ids
    low_g[4, mine] = jnp.where(keep, inverse_v[1], 0.0)
    window_start(low_g, LOW)
    low0_v[mine] = jnp.where(keep, inverse_v[0], 0.0)

    @pl.when(k == 1)
    def _():
        remote(low0_v.at[mine], low0_v.at[mine], LOW0, r, other)

    loads[0].wait()
    part1[...] = left_product(1)
    to_reducers(part1, red1, RED1, True)
    loads[4].wait()
    remote(panel_v.at[k], panel_v.at[k], PANEL, r, other)
    loads[1].wait()

    @pl.when(k == 0)
    def _():
        for b in range(2):
            diag_t[b] = chunks(diag_v[b])
        pl.semaphore_wait(passed_sem.at[0], 2)
        pass_on(1, 4)
        received(31, RED0)
        res0[q] = diag_t[0, q] - tree_sum(red0[i] for i in range(32))
        from_reducer(res0, RES0)
        received(8, LOW0)
        high, low = split(low0_v[...].T)
        window_hand_on(sub_g, SUB)
        window_hand_on(low_g, LOW)
        received(15, RES0)

        res_h, res_l = split(jnp.concatenate([res0[i] for i in range(16)], axis=0))
        both = dot(jnp.concatenate([res_h, res_l], axis=0), high)
        first_s[...] = (both[:128] + both[128:] + dot(res_h, low)).reshape(8, 2, 8, 128)
        pl.semaphore_wait(passed_sem.at[1], 2)
        for d in FAR_Z:
            remote(first_s.at[zs[d] % 8], first_z.at[d], FIRST, zs[d], c)

        received(48, SUB + 1)
        received(48, LOW + 1)
        received(31, RED1)
        chunk = diag_t[1, q] - tree_sum(red1[i] for i in range(32))

        @pl.when(away)
        def _():
            res1[...] = chunk
            remote(res1, res1_in, RES1, dst_row, 2 * dst_chip)

        @pl.when(jnp.logical_not(away))
        def _():
            res1_in[...] = chunk

        for w in range(WINDOW):
            high, low = split(sub_g[w])
            sub_h[:, 128 * w:128 * (w + 1)] = high
            sub_l[:, 128 * w:128 * (w + 1)] = low
        for w in range(WINDOW):
            low1_w[128 * w:128 * (w + 1), :] = jnp.concatenate(split(low_g[w].T), axis=1)

    received(128, PANEL)
    for i in range(8):
        highs, lows = [], []
        for b in range(2):
            cols = slice(128 * i, 128 * (i + 1))
            high, low = split(jnp.concatenate([panel_v[0, b, :, cols], panel_v[1, b, :, cols]], axis=0).T)
            highs.append(high)
            lows.append(low)
        panel_w[4 * i:4 * (i + 1)] = jnp.concatenate(highs + lows, axis=1).reshape(4, 32, 512)

    @pl.when(k == 0)
    def _():
        received(30, FIRST)
        first = first_s[group] + tree_sum(first_z[d] for d in range(1, NZ))
        place = pl.ds(2 * (group % 4), 2)
        first_o[...] = first

        high, low = split(first.reshape(16, 128))
        both = dot(jnp.concatenate([high, low], axis=0), sub_h[...])
        update = both[:16] + both[16:] + dot(high, sub_l[...])
        for w in range(WINDOW):
            for h in range(2):
                upd_s[2 * w + h] = update[8 * h:8 * (h + 1), 128 * w:128 * (w + 1)]
        to_reducers(upd_s, upd_r, UPDATE, False)

        for w in (0, 1, 7, 2, 6, 3, 5):
            remote(first_o, first_g.at[place], GROUP, zs[(4 - w) % NZ], 2 * q + half)

        @pl.when(half == 1)
        def _():
            remote(first_o, first_g.at[place], GROUP, r, c + 1)

        @pl.when(half == 0)
        def _():
            first_g[place] = first

        @pl.when(away)
        def _():
            sent(1, RES1)
            received(1, RES1)

        received(15, UPDATE)
        x_t[q] = res1_in[...] - tree_sum(upd_r[i] for i in range(16))
        from_reducer(x_t, SOLVE)
        sent(15, RED0)
        sent(15, RED1)
        sent(15, RES0)
        sent(30, FIRST)
        sent(32, SUB)
        sent(48, SUB + 1)
        sent(32, LOW)
        sent(48, LOW + 1)
        received(15, SOLVE)

        upper = jnp.concatenate([x_t[2 * w] for w in range(WINDOW)], axis=1)
        under = jnp.concatenate([x_t[2 * w + 1] for w in range(WINDOW)], axis=1)
        high, low = split(jnp.concatenate([upper, under], axis=0))
        both = dot(jnp.concatenate([high, low], axis=0), low1_w[...])
        second = (both[:16, :128] + both[16:, :128] + both[:16, 128:]).reshape(2, 8, 128)
        second_s[...] = second
        place = pl.ds(8 * (r // 8) + 2 * (group % 4), 2)
        for d in FAR_Z:
            remote(second_s, second_z.at[place], SECOND, zs[d], 2 * q + half)

        @pl.when(half == 1)
        def _():
            remote(second_s, second_z.at[place], SECOND, r, c + 1)
            sent(16, GROUP)
            sent(32, SECOND)

        @pl.when(half == 0)
        def _():
            second_z[place] = second
            sent(14, GROUP)
            sent(30, SECOND)

        sent(15, UPDATE)
        sent(15, SOLVE)

    @pl.when(k == 1)
    def _():
        sent(16, RED0)
        sent(16, RED1)
        sent(40, SUB)
        sent(40, LOW)
        sent(8, LOW0)

    own = jnp.logical_and(k == 0, half == 0)

    @pl.when(own)
    def _():
        received(6, GROUP)
        received(14, SECOND)

    @pl.when(jnp.logical_not(own))
    def _():
        received(8, GROUP)
        received(16, SECOND)

    turned = jnp.concatenate(
        [first_g[i] for i in range(8)] + [second_z[i] + second_z[8 + i] for i in range(8)], axis=0
    ).T
    lane = lax.broadcasted_iota(jnp.int32, (128, 128), 1) < 64
    high = turned.astype(BF16).astype(F32)
    low = turned - high
    high_r, low_r = pltpu.roll(high, 64, 1), pltpu.roll(low, 64, 1)
    weights = jnp.concatenate(
        [
            jnp.where(lane, high, low_r), jnp.where(lane, high_r, low),
            jnp.where(lane, high, 0.0), jnp.where(lane, high_r, 0.0),
        ],
        axis=0,
    ).astype(BF16)

    packed_half = lax.broadcasted_iota(jnp.int32, (16, 128), 1) < 64
    for i in range(4):
        part = CHIPS[4 * i:4 * (i + 1)]
        lines = jnp.concatenate([panel_w[2 * chip(o) + e] for o in part for e in range(2)], axis=0)
        wide = dot(lines, weights)
        wide = (wide + pltpu.roll(wide, 64, 1)).reshape(8, 2, 16, 128)
        for j, o in enumerate(part):
            slot = 2 * (4 * o[0] + o[1])
            for e in range(2):
                packed = jnp.where(packed_half, wide[2 * j + e, 0], wide[2 * j + e, 1])
                trail_s[slot + e] = packed
                if slot:
                    remote(trail_s.at[slot + e], trail_r.at[slot + k], TRAIL, r, 2 * chip(o) + e)
    remote(trail_s.at[1 - k], trail_r.at[k], TRAIL, r, other)
    trail_r[k] = trail_s[k]

    rows_s[...] = turned
    remote(rows_s.at[theirs], rows_r, ROWS, r, other)
    narrow = lax.broadcasted_iota(jnp.int32, (64, 128), 1) < 64
    sent(128, PANEL)
    received(8, ROWS)
    here, there = rows_s[mine], rows_r[...]
    lower = jnp.where(k == 0, here, there)
    upper = jnp.where(k == 0, there, here)
    solved_ref[0] = jnp.where(narrow, lower, pltpu.roll(upper, 64, 1))
    solved_ref[1] = jnp.where(narrow, pltpu.roll(lower, 64, 1), upper)
    sent(8, ROWS)
    received(62, TRAIL)
    lower = tree_sum(trail_r[2 * i] for i in range(16))
    upper = tree_sum(trail_r[2 * i + 1] for i in range(16))
    share_ref[:16] = jnp.where(packed_half, lower, pltpu.roll(upper, 64, 1))
    share_ref[16:] = jnp.where(packed_half, pltpu.roll(lower, 64, 1), upper)
    sent(62, TRAIL)


def on_device(*args):
    left, prior, diag, inverse, sub, panel = (
        pltpu.with_memory_space_constraint(a, pltpu.HBM) for a in args[:6]
    )
    tiles = lambda *n: pltpu.VMEM((*n, 8, 128), F32)
    solved, share = pl.pallas_call(
        kernel,
        out_shape=(jax.ShapeDtypeStruct((2, 64, 128), F32), jax.ShapeDtypeStruct((32, 128), F32)),
        in_specs=[pl.BlockSpec(memory_space=pltpu.HBM)] * 6,
        out_specs=(pl.BlockSpec(memory_space=pltpu.VMEM), pl.BlockSpec(memory_space=pltpu.VMEM)),
        scratch_shapes=[
            pltpu.VMEM((2, 128, 2048), F32),
            pltpu.VMEM((2048, 128), F32),
            pltpu.VMEM((2, 128, 128), F32),
            pltpu.VMEM((2, 64, 128), F32),
            pltpu.VMEM((WINDOW, 128, 128), F32),
            pltpu.VMEM((WINDOW, 128, 128), F32),
            pltpu.VMEM((128, 128), F32),
            pltpu.VMEM((2, 2, 64, 1024), F32),
            pltpu.VMEM((2048, 256), BF16),
            tiles(2, 16),
            tiles(16),
            tiles(16),
            tiles(32),
            tiles(32),
            tiles(16),
            tiles(),
            tiles(),
            tiles(8, 2),
            tiles(16, 2),
            tiles(2),
            tiles(8),
            pltpu.VMEM((128, 1024), BF16),
            pltpu.VMEM((128, 1024), BF16),
            tiles(16),
            tiles(16),
            tiles(16),
            pltpu.VMEM((1024, 256), BF16),
            tiles(2),
            tiles(16),
            pltpu.VMEM((32, 32, 512), BF16),
            pltpu.VMEM((128, 128), F32),
            pltpu.VMEM((64, 128), F32),
            pltpu.VMEM((32, 16, 128), F32),
            pltpu.VMEM((32, 16, 128), F32),
            pltpu.SemaphoreType.DMA((5,)),
            pltpu.SemaphoreType.DMA((2, CHUNKS)),
            pltpu.SemaphoreType.DMA((17,)),
            pltpu.SemaphoreType.DMA((17,)),
            pltpu.SemaphoreType.REGULAR((2,)),
        ],
        compiler_params=pltpu.CompilerParams(
            collective_id=0, has_side_effects=True, vmem_limit_bytes=32 * 1024 * 1024
        ),
    )(left, prior, diag, inverse, sub, panel)
    return solved, args[6] - share


def solution(mesh):
    in_specs = (
        P(None, "row", "col"),
        P("col", None),
        P(None, "row", None),
        P(None, "col", "row"),
        P("col", "row"),
        P(None, "col", "row"),
        P(("row", "col"), None),
    )
    out_specs = (P(None, "col", None), P(("row", "col"), None))
    return jax.shard_map(
        on_device, mesh=mesh, in_specs=in_specs, out_specs=out_specs, check_vma=False
    )
```

time: 492 us -> 58.5 us (0.12)
  waiting for transfers between devices: 379 us -> 0 us
  blocking collectives: 86.7 us -> 0 us
  Pallas kernels: 0 us -> 56.4 us
  between operations: 13.9 us -> 0.66 us
  matrix products: 7.41 us -> 0 us
    psum x2 -> x0, waiting for transfers between devices: 272 us -> none  [the longest x1 136 us: on_device(): update = lax.psum(sub_partial, 'col')]
    unnamed x4 -> x0, waiting for transfers between devices: 107 us -> none
    psum x2 -> x0, blocking collectives: 86.7 us -> none  [solve_block(): return lax.psum(partial_solve, 'row')]
    pallas_call x0 -> x1, Pallas kernels: none -> 56.4 us  [on_device(): pl.pallas_call(kernel, out_shape=(jax.ShapeDtypeStruct((2, 64, 128), F32)...]
    dot_general x5 -> x0, matrix products: 7.41 us -> none  [the longest x1 3.68 us: on_device(): jnp.einsum('knj,jr->knr', left_rows, prior_solution, precision=precise)]
  transfers between devices with their start and end apart: 3 -> 0, of which waited for: 3 -> 0; matrix products, arithmetic and copies ran while one was open for 0% -> 0% of each run, Pallas kernels for 0% -> 0%
where the time goes in v4:
time: 58.5 us; the launch traced here: 58.3 us
  Pallas kernels  56.4 us (96%)
  between operations  0.66 us (1%)
  local copies, waits for them, and re-layouts  0.63 us (1%)
  other arithmetic  0.61 us (1%)
    pallas_call x1, Pallas kernels, on_device(): pl.pallas_call(kernel, out_shape=(jax.ShapeDtypeStruct((2, 64, 128), F32)...  56.4 us

profile of v4, /device:TPU:1, one launch (start us, length us, event | category | flops | bytes accessed | tf_op | source)
XLA Modules:
  0.0 58.3 jit_solution(13205204313351229183)
XLA Ops:
  0.6 0.0 copy-start
  0.6 56.4 %shard_map.86 = (f32[2,64,128]{2,1,0:T(8,128)S(1)}, f32[32,128]{1,0:T(8,128)S(1)}) custom-call(f32[2,128,2048]{2,1,0:T(8,128)} %left.1, f32[2048,128]{1,0:T(8,128)} %prior.1, f32[2,128,128]{2,1,0:T(8,128)} %diag.1, f32[2,64,128]{2,1,0:T(8,128)} %inverse.1, f32[64,128]{1,0:T(8,128)} %sub.5, f32[2,64,1024]{2,1,0:T(8,128)} %panel.1), custom_call_target="tpu_custom_call" | custom-call | tf_op jit(solution)/shard_map/pallas_call | solution.py:403
  57.0 0.0 copy-done
  57.1 0.6 %sub.4 = f32[32,128]{1,0:T(8,128)} subtract(f32[32,128]{1,0:T(8,128)S(1)} %copy-done, f32[32,128]{1,0:T(8,128)S(1)} %get-tuple-element.5) | non-fusion elementwise | flops 4096 | bytes 49152 | tf_op jit(solution)/shard_map/sub | solution.py:453
  57.7 0.6 %copy.10 = f32[2,64,128]{2,1,0:T(8,128)} copy(f32[2,64,128]{2,1,0:T(8,128)S(1)} %get-tuple-element.8) | data formatting | bytes 131072
Async XLA Ops:
  0.6 56.4 %copy-start = (f32[32,128]{1,0:T(8,128)S(1)}, f32[32,128]{1,0:T(8,128)}, u32[]{:S(2)}) copy-start(f32[32,128]{1,0:T(8,128)} %param.13) | copy-start | bytes 49156

commit v5 on v3

--- a/solution.py
+++ b/solution.py
@@ -10,7 +10,7 @@
 BF16 = jnp.bfloat16
 MESH = pl.DeviceIdType.MESH
 NZ = 16
-CHUNKS = 4
+CHUNKS = 2
 WINDOW = 8
 SUB, LOW = 13, 15
 
@@ -168,13 +168,14 @@
                 pltpu.make_async_copy(prior.at[rows, :], prior_v.at[rows, :], chunk_sem.at[0, i]).wait()
                 prior_w[rows, :] = jnp.concatenate(split(prior_v[rows, :]), axis=1)
                 pltpu.make_async_copy(left.at[0, :, rows], left_v.at[0, :, rows], chunk_sem.at[1, i]).wait()
-            high, low = split(left_v[b, :, rows])
-            wide = dot(high, prior_w[rows, :])
-            term = wide[:, :128] + wide[:, 128:] + dot(low, prior_w[rows, :128])
-            total = term if total is None else total + term
-        return total.T.reshape(16, 8, 128)
-
-    part0[...] = left_product(0, range(CHUNKS))
+            wide = dot(jnp.concatenate(split(left_v[b, :, rows]), axis=0), prior_w[rows, :])
+            total = wide if total is None else total + wide
+        return total[:128, :128] + total[:128, 128:] + total[128:, :128]
+
+    def chunks(product):
+        return product.T.reshape(16, 8, 128)
+
+    part0[...] = chunks(left_product(0, range(CHUNKS)))
 
     pl.semaphore_wait(barrier, 39)
 
@@ -203,7 +204,7 @@
     low0_l[...] = low
 
     loads[0].wait()
-    part1[...] = left_product(1, range(CHUNKS))
+    diag_v[...] = left_product(1, range(CHUNKS // 2))
 
     @pl.when(k == 0)
     def _():
@@ -211,6 +212,7 @@
         res0[q] = diag_t[q] - tree_sum(red0[i] for i in range(32))
         from_reducer(res0, 0, 2)
 
+    part1[...] = chunks(diag_v[...] + left_product(1, range(CHUNKS // 2, CHUNKS)))
     to_reducers(part1, red1, 1, 1)
     window_hand_on(sub_g, SUB)
     window_hand_on(low_g, LOW)
@@ -227,21 +229,6 @@
         remote(first_s.at[zs[d] % 8], first_z.at[d], 5, zs[d], c)
     group = r % 8
 
-    @pl.when(k == 1)
-    def _():
-        received(red1.at[pl.ds(0, 31)], 1)
-        mine = diag_t[q] - tree_sum(red1[i] for i in range(32))
-
-        @pl.when(away)
-        def _():
-            res1[...] = mine
-            remote(res1, res1_in, 3, dst_row, 2 * dst_chip + 1)
-
-        @pl.when(jnp.logical_not(away))
-        def _():
-            res1_in[...] = mine
-
-    to_reducers_sent(part1, 1, 1)
     loads[4].wait()
     for i in range(8):
         block = panel_v[:, :, 128 * i:128 * (i + 1)].reshape(128, 128).T
@@ -256,6 +243,22 @@
         high, low = split(low_g[w])
         stacked = jnp.concatenate([high.astype(F32), low.astype(F32)], axis=0).T
         low1_w[128 * w:128 * (w + 1), :] = stacked.astype(BF16)
+
+    @pl.when(k == 1)
+    def _():
+        received(red1.at[pl.ds(0, 31)], 1)
+        mine = diag_t[q] - tree_sum(red1[i] for i in range(32))
+
+        @pl.when(away)
+        def _():
+            res1[...] = mine
+            remote(res1, res1_in, 3, dst_row, 2 * dst_chip + 1)
+
+        @pl.when(jnp.logical_not(away))
+        def _():
+            res1_in[...] = mine
+
+    to_reducers_sent(part1, 1, 1)
 
     @pl.when(k == 0)
     def _():

time: 57.9 us -> 58 us (level)
  no operation moved by 1% of the time
where the time goes in v5:
time: 58 us; the launch traced here: 57.8 us
  Pallas kernels  55.9 us (96%)
  between operations  0.66 us (1%)
  local copies, waits for them, and re-layouts  0.63 us (1%)
  other arithmetic  0.61 us (1%)
    pallas_call x1, Pallas kernels, on_device(): pl.pallas_call(kernel, out_shape=(jax.ShapeDtypeStruct((2, 64, 128), F32)...  55.9 us

profile of v5, /device:TPU:1, one launch (start us, length us, event | category | flops | bytes accessed | tf_op | source)
XLA Modules:
  0.0 57.8 jit_solution(2895746811677892533)
XLA Ops:
  0.6 0.0 copy-start
  0.6 55.9 %shard_map.86 = (f32[2,64,128]{2,1,0:T(8,128)S(1)}, f32[32,128]{1,0:T(8,128)S(1)}) custom-call(f32[2,128,2048]{2,1,0:T(8,128)} %left.1, f32[2048,128]{1,0:T(8,128)} %prior.1, f32[2,128,128]{2,1,0:T(8,128)} %diag.1, f32[2,64,128]{2,1,0:T(8,128)} %inverse.1, f32[64,128]{1,0:T(8,128)} %sub.5, f32[2,64,1024]{2,1,0:T(8,128)} %panel.1), custom_call_target="tpu_custom_call" | custom-call | tf_op jit(solution)/shard_map/pallas_call | solution.py:363
  56.6 0.0 copy-done
  56.6 0.6 %sub.4 = f32[32,128]{1,0:T(8,128)} subtract(f32[32,128]{1,0:T(8,128)S(1)} %copy-done, f32[32,128]{1,0:T(8,128)S(1)} %get-tuple-element.5) | non-fusion elementwise | flops 4096 | bytes 49152 | tf_op jit(solution)/shard_map/sub | solution.py:413
  57.2 0.6 %copy.10 = f32[2,64,128]{2,1,0:T(8,128)} copy(f32[2,64,128]{2,1,0:T(8,128)S(1)} %get-tuple-element.8) | data formatting | bytes 131072
Async XLA Ops:
  0.6 56.0 %copy-start = (f32[32,128]{1,0:T(8,128)S(1)}, f32[32,128]{1,0:T(8,128)}, u32[]{:S(2)}) copy-start(f32[32,128]{1,0:T(8,128)} %param.13) | copy-start | bytes 49156
